TPU v7x, 32 devices: a whole 2x2x4 slice. The times are simulated.
32 devices in a mesh: freq: 2 (over x), tm: 8 (over z, core), batch: 2 (over y).
Axes of the slice: x: 2, y: 2, z: 4, core: 2. Of those that a mesh axis runs over, the one named last changes fastest.
Arguments:
- patches: bfloat16 [16, 8, 256, 384], P('batch', 'freq', 'tm'), may hold values from -6 to 6
- patch_mask: int32 [16, 8, 256], P('batch', 'freq', 'tm'), may hold values 0 or 1
- clip_lengths: int32 [16], P('batch'), may hold values from 1 to 256
- target_index: int32 [16, 8, 256], P('batch', 'freq', 'tm'), may hold values from 0 to 127
- targets: bfloat16 [16, 128, 384], P('batch'), may hold values from -0.41992188 to 0.41992188
- out_grad: bfloat16 [16, 8, 256, 384], P('batch', 'freq', 'tm'), may hold values from -6 to 6
- mask_embed: bfloat16 [384], replicated, may hold values from -4 to 4
- ln1_gain: bfloat16 [384], replicated, may hold values from 0.25 to 1.75
- ln1_shift: bfloat16 [384], replicated, may hold values from -1.5 to 1.5
- w_qkv: bfloat16 [384, 1152], replicated, may hold values from -0.3125 to 0.3125
- bias_q: bfloat16 [384], replicated, may hold values from -1.5 to 1.5
- bias_v: bfloat16 [384], replicated, may hold values from -0.25 to 0.25
- w_out: bfloat16 [384, 384], replicated, may hold values from -1.5 to 1.5
- bias_out: bfloat16 [384], replicated, may hold values from -1.5 to 1.5
- ln2_gain: bfloat16 [384], replicated, may hold values from 0.25 to 1.75
- ln2_shift: bfloat16 [384], replicated, may hold values from -1.5 to 1.5
- w_up: bfloat16 [384, 1536], replicated, may hold values from -0.3125 to 0.3125
- bias_up: bfloat16 [1536], replicated, may hold values from -1.5 to 1.5
- w_down: bfloat16 [1536, 384], replicated, may hold values from -0.15625 to 0.15625
- bias_down: bfloat16 [384], replicated, may hold values from -1.5 to 1.5
Outputs:
- block_out: bfloat16 [16, 8, 256, 384], P('batch', 'freq', 'tm')
- input_grad: bfloat16 [16, 8, 256, 384], P('batch', 'freq', 'tm')
- grad_mask_embed: float32 [384], replicated
- grad_ln1_gain: float32 [384], replicated
- grad_ln1_shift: float32 [384], replicated
- grad_w_qkv: float32 [384, 1152], replicated
- grad_bias_q: float32 [384], replicated
- grad_bias_v: float32 [384], replicated
- grad_w_out: float32 [384, 384], replicated
- grad_bias_out: float32 [384], replicated
- grad_ln2_gain: float32 [384], replicated
- grad_ln2_shift: float32 [384], replicated
- grad_w_up: float32 [384, 1536], replicated
- grad_bias_up: float32 [1536], replicated
- grad_w_down: float32 [1536, 384], replicated
- grad_bias_down: float32 [384], replicated
- soft_accuracy: float32 [16], P('batch')
All inputs are finite; a program needn't handle non-finite values. No bound on the sum of `patch_mask` on one device may be relied on, other than what follows from the above.
Results may differ from a plain program's by a relative error of at most 0.014.
Values may be sent and summed in bfloat16 or wider, within the bound.
A program may use at most 256 MiB of HBM per device.

v0:
```python
import jax
import jax.numpy as jnp
from jax import lax
from jax.sharding import PartitionSpec as P

D = 384
HEADS = 6
HEAD_DIM = 64
BLOCK_CLIPS = 4


def layer_norm(inputs, gain_vec, shift_vec):
    center = inputs - jnp.mean(inputs, axis=-1, keepdims=True)
    spread = jnp.mean(center * center, axis=-1, keepdims=True)
    return center * lax.rsqrt(spread + 1e-06) * gain_vec + shift_vec


def gelu_exact(inputs):
    return jax.nn.gelu(inputs, approximate=False)


def inner_rows(left_mat, right_mat):
    return lax.dot_general(
        left_mat, right_mat, (((0,), (0,)), ((), ())), preferred_element_type=jnp.float32
    )


def times_transpose(left_mat, right_mat):
    return lax.dot_general(
        left_mat, right_mat, (((1,), (1,)), ((), ())), preferred_element_type=jnp.float32
    )


def gather_keys(local):
    wider = lax.all_gather(local, "freq", axis=1, tiled=True)
    return lax.all_gather(wider, "tm", axis=2, tiled=True)


def gather_again(local):
    wider = lax.all_gather(local, "freq", axis=1, tiled=True)
    return lax.all_gather(wider, "tm", axis=2, tiled=True)


def split_heads(full_kv):
    blocks = full_kv.shape[0]
    flat_rows = full_kv.reshape(blocks, -1, 2 * D)
    key_rows = flat_rows[:, :, :D].reshape(blocks, -1, HEADS, HEAD_DIM)
    value_rows = flat_rows[:, :, D:].reshape(blocks, -1, HEADS, HEAD_DIM)
    return (key_rows, value_rows)


def masked_scores(queries, key_rows, lengths, full_kv):
    scores = jnp.einsum(
        "bqhd,bkhd->bhqk", queries, key_rows, preferred_element_type=jnp.float32
    ) * HEAD_DIM ** (-0.5)
    positions = lax.broadcasted_iota(
        jnp.int32, (full_kv.shape[0], full_kv.shape[1], full_kv.shape[2]), 2
    )
    usable = (positions < lengths[:, None, None]).reshape(full_kv.shape[0], -1)
    return jnp.where(usable[:, None, None, :], scores, -1000000000.0)


def attend_forward(queries, full_kv, lengths):
    key_rows, value_rows = split_heads(full_kv)
    scores = masked_scores(queries, key_rows, lengths, full_kv)
    row_max = jnp.max(scores, axis=-1, keepdims=True)
    raised = jnp.exp(scores - row_max)
    row_total = jnp.sum(raised, axis=-1, keepdims=True)
    attn_prob = (raised / row_total).astype(jnp.bfloat16)
    mixed = jnp.einsum("bhqk,bkhd->bqhd", attn_prob, value_rows, preferred_element_type=jnp.float32)
    return (mixed.astype(jnp.bfloat16), row_max + jnp.log(row_total))


def attend_backward(queries, full_kv, lengths, grad_mixed, log_total):
    key_rows, value_rows = split_heads(full_kv)
    scores = masked_scores(queries, key_rows, lengths, full_kv)
    attn_prob = jnp.exp(scores - log_total)
    grad_prob = jnp.einsum(
        "bqhd,bkhd->bhqk", grad_mixed, value_rows, preferred_element_type=jnp.float32
    )
    center = jnp.sum(attn_prob * grad_prob, axis=-1, keepdims=True)
    grad_scores = (attn_prob * (grad_prob - center)).astype(jnp.bfloat16)
    scale = HEAD_DIM ** (-0.5)
    grad_queries = (
        jnp.einsum("bhqk,bkhd->bqhd", grad_scores, key_rows, preferred_element_type=jnp.float32)
        * scale
    )
    grad_keys = (
        jnp.einsum("bhqk,bqhd->bkhd", grad_scores, queries, preferred_element_type=jnp.float32)
        * scale
    )
    grad_values = jnp.einsum(
        "bhqk,bqhd->bkhd",
        attn_prob.astype(jnp.bfloat16),
        grad_mixed,
        preferred_element_type=jnp.float32,
    )
    blocks = full_kv.shape[0]
    grad_full = jnp.concatenate(
        [grad_keys.reshape(blocks, -1, D), grad_values.reshape(blocks, -1, D)], axis=-1
    )
    grad_full = grad_full.reshape(full_kv.shape)
    own_part = lax.psum_scatter(
        grad_full.astype(jnp.bfloat16), "tm", scatter_dimension=2, tiled=True
    ).astype(jnp.float32)
    own_part = lax.psum_scatter(
        own_part.astype(jnp.bfloat16), "freq", scatter_dimension=1, tiled=True
    ).astype(jnp.float32)
    return (grad_queries.astype(jnp.bfloat16), own_part.astype(jnp.bfloat16))


def per_device(
    patches,
    patch_mask,
    clip_lengths,
    target_index,
    targets,
    out_grad,
    mask_embed,
    ln1_gain,
    ln1_shift,
    w_qkv,
    bias_q,
    bias_v,
    w_out,
    bias_out,
    ln2_gain,
    ln2_shift,
    w_up,
    bias_up,
    w_down,
    bias_down,
):
    clips, freq_rows, time_rows, width = patches.shape
    clip_rows = freq_rows * time_rows
    tokens = clips * clip_rows
    groups = clips // BLOCK_CLIPS
    masked = (patch_mask == 1)[..., None]
    flat_mask = masked.reshape(tokens, 1)
    start = jnp.where(masked, mask_embed.astype(jnp.float32), patches.astype(jnp.float32)).reshape(
        tokens, width
    )
    normed, first_back = jax.vjp(
        layer_norm, start, ln1_gain.astype(jnp.float32), ln1_shift.astype(jnp.float32)
    )
    normed_low = normed.astype(jnp.bfloat16)
    project = jnp.dot(normed_low, w_qkv, preferred_element_type=jnp.float32)
    queries = (project[:, :D] + bias_q.astype(jnp.float32)).astype(jnp.bfloat16)
    key_part = project[:, D : 2 * D]
    value_part = project[:, 2 * D :] + bias_v.astype(jnp.float32)
    local_kv = jnp.concatenate([key_part, value_part], axis=-1).astype(jnp.bfloat16)
    local_kv = local_kv.reshape(groups, BLOCK_CLIPS, freq_rows, time_rows, 2 * D)
    query_blocks = queries.reshape(groups, BLOCK_CLIPS, clip_rows, HEADS, HEAD_DIM)
    length_blocks = clip_lengths.reshape(groups, BLOCK_CLIPS)

    def forward_block(element):
        full_kv = gather_keys(element[1])
        return attend_forward(element[0], full_kv, element[2])

    mixed, log_total = lax.map(forward_block, (query_blocks, local_kv, length_blocks))
    mixed_rows = mixed.reshape(tokens, D)
    middle = (
        start
        + jnp.dot(mixed_rows, w_out, preferred_element_type=jnp.float32)
        + bias_out.astype(jnp.float32)
    )
    second, second_back = jax.vjp(
        layer_norm, middle, ln2_gain.astype(jnp.float32), ln2_shift.astype(jnp.float32)
    )
    second_low = second.astype(jnp.bfloat16)
    hidden_up = jnp.dot(second_low, w_up, preferred_element_type=jnp.float32) + bias_up.astype(
        jnp.float32
    )
    activated_f, gelu_back = jax.vjp(gelu_exact, hidden_up)
    activated = activated_f.astype(jnp.bfloat16)
    result = (
        middle
        + jnp.dot(activated, w_down, preferred_element_type=jnp.float32)
        + bias_down.astype(jnp.float32)
    )
    block_out = result.astype(jnp.bfloat16)
    grad_down = out_grad.reshape(tokens, width)
    grad_w_down = inner_rows(activated, grad_down)
    grad_bias_down = jnp.sum(grad_down.astype(jnp.float32), axis=0)
    grad_act = times_transpose(grad_down, w_down)
    grad_up = gelu_back(grad_act)[0].astype(jnp.bfloat16)
    grad_w_up = inner_rows(second_low, grad_up)
    grad_bias_up = jnp.sum(grad_up.astype(jnp.float32), axis=0)
    grad_second = times_transpose(grad_up, w_up)
    grad_middle_norm, grad_ln2_gain, grad_ln2_shift = second_back(grad_second)
    grad_middle = grad_down.astype(jnp.float32) + grad_middle_norm
    grad_branch = grad_middle.astype(jnp.bfloat16)
    grad_w_out = inner_rows(mixed_rows, grad_branch)
    grad_bias_out = jnp.sum(grad_branch.astype(jnp.float32), axis=0)
    grad_mixed = times_transpose(grad_branch, w_out).astype(jnp.bfloat16)
    grad_mixed = grad_mixed.reshape(groups, BLOCK_CLIPS, clip_rows, HEADS, HEAD_DIM)

    def backward_block(element):
        full_kv = gather_again(element[1])
        return attend_backward(element[0], full_kv, element[2], element[3], element[4])

    grad_queries, grad_kv = lax.map(
        backward_block, (query_blocks, local_kv, length_blocks, grad_mixed, log_total)
    )
    grad_query_rows = grad_queries.reshape(tokens, D)
    grad_kv_rows = grad_kv.reshape(tokens, 2 * D)
    grad_project = jnp.concatenate([grad_query_rows, grad_kv_rows], axis=-1)
    grad_w_qkv = inner_rows(normed_low, grad_project)
    grad_bias_q = jnp.sum(grad_query_rows.astype(jnp.float32), axis=0)
    grad_bias_v = jnp.sum(grad_kv_rows[:, D:].astype(jnp.float32), axis=0)
    grad_normed = times_transpose(grad_project, w_qkv)
    grad_start_norm, grad_ln1_gain, grad_ln1_shift = first_back(grad_normed)
    grad_start = grad_middle + grad_start_norm
    grad_mask_embed = jnp.sum(jnp.where(flat_mask, grad_start, 0.0), axis=0)
    input_grad = jnp.where(flat_mask, 0.0, grad_start).astype(jnp.bfloat16).reshape(patches.shape)
    summed = lax.psum(
        (
            grad_mask_embed,
            grad_ln1_gain,
            grad_ln1_shift,
            grad_w_qkv,
            grad_bias_q,
            grad_bias_v,
            grad_w_out,
            grad_bias_out,
            grad_ln2_gain,
            grad_ln2_shift,
            grad_w_up,
            grad_bias_up,
            grad_w_down,
            grad_bias_down,
        ),
        ("freq", "tm", "batch"),
    )
    out_rows = block_out.reshape(clips, clip_rows, width)
    logits = jnp.einsum("cqd,cnd->cqn", out_rows, targets, preferred_element_type=jnp.float32)
    logit_max = jnp.max(logits, axis=-1, keepdims=True)
    raised = jnp.exp(logits - logit_max)
    cand_prob = raised / jnp.sum(raised, axis=-1, keepdims=True)
    cand_ids = lax.broadcasted_iota(jnp.int32, cand_prob.shape, 2)
    picked = jnp.sum(
        jnp.where(cand_ids == target_index.reshape(clips, clip_rows)[..., None], cand_prob, 0.0),
        axis=-1,
    )
    positions = lax.axis_index("tm") * time_rows + lax.broadcasted_iota(
        jnp.int32, (clips, freq_rows, time_rows), 2
    )
    live_rows = (
        ((patch_mask == 1) & (positions < clip_lengths[:, None, None]))
        .reshape(clips, clip_rows)
        .astype(jnp.float32)
    )
    prob_sum, counted = lax.psum(
        (jnp.sum(picked * live_rows, axis=1), jnp.sum(live_rows, axis=1)), ("freq", "tm")
    )
    soft_accuracy = prob_sum / jnp.maximum(counted, 1.0)
    block_grid = block_out.reshape(patches.shape)
    return (
        block_grid,
        input_grad,
        summed[0],
        summed[1],
        summed[2],
        summed[3],
        summed[4],
        summed[5],
        summed[6],
        summed[7],
        summed[8],
        summed[9],
        summed[10],
        summed[11],
        summed[12],
        summed[13],
        soft_accuracy,
    )


def solution(mesh):
    in_specs = (
        P("batch", "freq", "tm", None),
        P("batch", "freq", "tm"),
        P("batch"),
        P("batch", "freq", "tm"),
        P("batch", None, None),
        P("batch", "freq", "tm", None),
        P(),
        P(),
        P(),
        P(),
        P(),
        P(),
        P(),
        P(),
        P(),
        P(),
        P(),
        P(),
        P(),
        P(),
    )
    out_specs = (
        P("batch", "freq", "tm", None),
        P("batch", "freq", "tm", None),
        P(),
        P(),
        P(),
        P(),
        P(),
        P(),
        P(),
        P(),
        P(),
        P(),
        P(),
        P(),
        P(),
        P(),
        P("batch"),
    )
    return jax.shard_map(
        per_device, mesh=mesh, in_specs=in_specs, out_specs=out_specs, check_vma=False
    )
```

profile of v0, /device:TPU:0, one launch (start us, length us, event | category | flops | bytes accessed | tf_op | source)
XLA Modules:
  0.0 1619.8 jit_solution(8345233267946131010)
XLA Ops:
  26.1 449.2 %while.24 = (s32[]{:T(128)}, bf16[2,4,128,6,64]{2,1,0,4,3:T(4,128)(2,1)}, f32[2,4,6,128,1]{3,2,1,4,0:T(8,128)}, bf16[2,4,4,32,768]{4,3,1,0,2:T(8,128)(2,1)S(1)},...) while((s32[]{:T(128)}, bf16[2,4,128,6,64]{2,1,0,4,3:T(4,128)(2,1)}, ...), condition=%wide.region_5.6_spmd, body=%wide.region_2.5_spmd.sunk | while | flops 1686311936 | bytes 244748528 | solution.py:160
  27.5 31.9 %all-gather.17.cloned.1.call-done = bf16[1,4,8,32,768]{4,3,1,0,2:T(8,128)(2,1)} async-done(((bf16[1,4,4,32,768]{4,3,1,0,2:T(8,128)(2,1)}), bf16[1,4,8,32,768]{4,3,1,0,2:T(8,128)(2,1)}) %all-gather.17.cloned.1.call-update) | async-done | bytes 1572880 | tf_op jit(solution)/shard_map/while/body/eval_jaxpr/all_gather | solution.py:35
  63.6 116.1 %all-gather.19.cloned.1.call-done = bf16[1,4,8,256,768]{4,2,1,0,3:T(8,128)(2,1)} async-done(((bf16[1,4,8,32,768]{4,2,1,0,3:T(8,128)(2,1)}), bf16[1,4,8,256,768]{4,2,1,0,3:T(8,128)(2,1)}) %all-gather.19.cloned.1.call-update) | async-done | bytes 12582928 | tf_op jit(solution)/shard_map/while/body/eval_jaxpr/all_gather | solution.py:36
  179.7 9.1 copy.128
  188.8 5.9 fusion.127
  194.7 8.6 copy.131
  203.3 8.7 copy.129
  212.0 14.7 fusion.129
  226.7 11.4 fusion.130
  238.7 12.2 fusion.131
  253.9 27.5 %all-gather.17.cloned.1.call-done = bf16[1,4,8,32,768]{4,3,1,0,2:T(8,128)(2,1)} async-done(((bf16[1,4,4,32,768]{4,3,1,0,2:T(8,128)(2,1)}), bf16[1,4,8,32,768]{4,3,1,0,2:T(8,128)(2,1)}) %all-gather.17.cloned.1.call-update) | async-done | bytes 1572880 | tf_op jit(solution)/shard_map/while/body/eval_jaxpr/all_gather | solution.py:35
  285.6 116.1 %all-gather.19.cloned.1.call-done = bf16[1,4,8,256,768]{4,2,1,0,3:T(8,128)(2,1)} async-done(((bf16[1,4,8,32,768]{4,2,1,0,3:T(8,128)(2,1)}), bf16[1,4,8,256,768]{4,2,1,0,3:T(8,128)(2,1)}) %all-gather.19.cloned.1.call-update) | async-done | bytes 12582928 | tf_op jit(solution)/shard_map/while/body/eval_jaxpr/all_gather | solution.py:36
  401.7 9.1 copy.128
  410.8 5.9 fusion.127
  416.6 8.6 copy.131
  425.2 8.7 copy.129
  434.0 14.7 fusion.129
  448.6 11.4 fusion.130
  460.6 12.2 fusion.131
  481.5 16.3 %multiply_convert_fusion.2 = (bf16[1024,1536]{1,0:T(8,128)(2,1)}, f32[1024,1536]{1,0:T(8,128)S(1)}, f32[1024,1536]{1,0:T(8,128)S(1)}) fusion(f32[1536]{0:T(1024)S(1)} %convert_element_type.124, bf16[384,1536]{1,0:T(8,128)(2,1)S(1)} %copy-done, f32[1024,384]{1,0:T(8,128)S(1)} %get-tuple-element.228, f32[384]{0:T(512)S(1)} %convert_element_type.122, ...), kind=kOutput, calls=%fused_computation.62 | convolution fusion | flops 1313734656 | bytes 18498560 | tf_op jit(solution)/shard_map/dot_general | solution.py:171
  497.7 4.3 convert_reduce_fusion
  515.6 912.0 %while.25 = (s32[]{:T(128)}, bf16[2,4,128,6,64]{2,4,3,1,0:T(8,128)(2,1)}, bf16[2,4,4,32,768]{4,3,2,1,0:T(8,128)(2,1)}, bf16[2,4,4,32,768]{4,3,1,0,2:T(8,128)(2,1...) while((s32[]{:T(128)}, ...), condition=%wide.region_14.15_spmd, body=%wide.region_10.14_spmd.sunk | while | flops 4155905024 | bytes 551883200 | solution.py:202
  521.1 27.0 %all-gather.21.cloned.1.call-done = bf16[1,4,8,32,768]{4,3,1,0,2:T(8,128)(2,1)} async-done(((bf16[1,4,4,32,768]{4,3,1,0,2:T(8,128)(2,1)}), bf16[1,4,8,32,768]{4,3,1,0,2:T(8,128)(2,1)}) %all-gather.21.cloned.1.call-update) | async-done | bytes 1572880 | tf_op jit(solution)/shard_map/while/body/eval_jaxpr/all_gather | solution.py:40
  553.2 115.2 %all-gather.23.cloned.1.call-done = bf16[1,4,8,256,768]{4,2,1,0,3:T(8,128)(2,1)} async-done(((bf16[1,4,8,32,768]{4,2,1,0,3:T(8,128)(2,1)}), bf16[1,4,8,256,768]{4,2,1,0,3:T(8,128)(2,1)}) %all-gather.23.cloned.1.call-update) | async-done | bytes 12582928 | tf_op jit(solution)/shard_map/while/body/eval_jaxpr/all_gather | solution.py:41
  668.4 9.1 copy.136
  677.5 5.6 fusion.141
  683.1 8.7 copy.137
  691.8 8.7 copy.139
  700.5 14.6 fusion.142
  715.0 12.9 fusion.145
  727.9 18.5 %multiply_reduce_fusion.8 = (f32[4,6,128]{2,1,0:T(8,128)S(1)}, f32[4,6,128,2048]{3,2,1,0:T(8,128)}) fusion(f32[4,6,128,2048]{3,2,1,0:T(8,128)} %fusion.142, f32[4,6,128]{2,1,0:T(8,128)S(1)} %copy-done.18, pred[4,2048]{1,0:T(4,128)(4,1)S(1)} %broadcast_compare_fusion.6, bf16[4,2048,6,64]{1,3,2,0:T(8,128)(2,1)} %bitcast.204, ...), kind=kOutput, calls=%fused_computation.22.clone.1 | convolution fusion | flops 836760576 | bytes 57049088 | tf_op jit(solution)/shard_map/while/body/eval_jaxpr/bqhd,bkhd->bhqk/dot_general | solution.py:78
  746.4 16.9 %multiply_convert_fusion.5 = bf16[4,6,128,2048]{3,2,1,0:T(8,128)(2,1)S(1)} fusion(f32[4,6,128,2048]{3,2,1,0:T(8,128)} %get-tuple-element.334, f32[4,6,128,2048]{3,2,1,0:T(8,128)} %fusion.142, f32[4,6,128]{2,1,0:T(8,128)S(1)} %get-tuple-element.335, f32[4,6,128]{2,1,0:T(8,128)S(1)} %copy-done.18, pred[4,2048]{1,0:T(4,128)(4,1)S(1)} %broadcast_compare_fusion.6), kind=kLoop, calls=%fused_computation.21.clone.1 | loop fusion | flops 37748736 | bytes 62947328 | tf_op jit(solution)/shard_map/while/body/eval_jaxpr/convert_element_type | solution.py:82
  767.9 5.3 copy.142
  773.2 9.7 copy.143
  782.9 8.1 copy.140
  791.0 9.7 copy.141
  800.8 10.6 pad_maximum_fusion.6
  811.4 127.6 %reduce-scatter.3.cloned.1.call-done = bf16[4,8,32,768]{3,1,0,2:T(8,128)(2,1)} async-done(((bf16[4,8,256,768]{3,1,0,2:T(8,128)(2,1)}), bf16[4,8,32,768]{3,1,0,2:T(8,128)(2,1)}) %reduce-scatter.3.cloned.1.call-update) | async-done | bytes 1572880 | tf_op jit(solution)/shard_map/while/body/eval_jaxpr/reduce_scatter | solution.py:103
  942.5 12.2 fusion.144
  954.7 12.3 reduce-scatter.5.cloned.1.call-done
  970.2 29.1 %all-gather.21.cloned.1.call-done = bf16[1,4,8,32,768]{4,3,1,0,2:T(8,128)(2,1)} async-done(((bf16[1,4,4,32,768]{4,3,1,0,2:T(8,128)(2,1)}), bf16[1,4,8,32,768]{4,3,1,0,2:T(8,128)(2,1)}) %all-gather.21.cloned.1.call-update) | async-done | bytes 1572880 | tf_op jit(solution)/shard_map/while/body/eval_jaxpr/all_gather | solution.py:40
  1004.5 115.2 %all-gather.23.cloned.1.call-done = bf16[1,4,8,256,768]{4,2,1,0,3:T(8,128)(2,1)} async-done(((bf16[1,4,8,32,768]{4,2,1,0,3:T(8,128)(2,1)}), bf16[1,4,8,256,768]{4,2,1,0,3:T(8,128)(2,1)}) %all-gather.23.cloned.1.call-update) | async-done | bytes 12582928 | tf_op jit(solution)/shard_map/while/body/eval_jaxpr/all_gather | solution.py:41
  1119.7 9.1 copy.136
  1128.8 5.6 fusion.141
  1134.4 8.7 copy.137
  1143.1 8.7 copy.139
  1151.7 14.6 fusion.142
  1166.3 12.9 fusion.145
  1179.2 18.5 %multiply_reduce_fusion.8 = (f32[4,6,128]{2,1,0:T(8,128)S(1)}, f32[4,6,128,2048]{3,2,1,0:T(8,128)}) fusion(f32[4,6,128,2048]{3,2,1,0:T(8,128)} %fusion.142, f32[4,6,128]{2,1,0:T(8,128)S(1)} %copy-done.18, pred[4,2048]{1,0:T(4,128)(4,1)S(1)} %broadcast_compare_fusion.6, bf16[4,2048,6,64]{1,3,2,0:T(8,128)(2,1)} %bitcast.204, ...), kind=kOutput, calls=%fused_computation.22.clone.1 | convolution fusion | flops 836760576 | bytes 57049088 | tf_op jit(solution)/shard_map/while/body/eval_jaxpr/bqhd,bkhd->bhqk/dot_general | solution.py:78
  1197.7 16.9 %multiply_convert_fusion.5 = bf16[4,6,128,2048]{3,2,1,0:T(8,128)(2,1)S(1)} fusion(f32[4,6,128,2048]{3,2,1,0:T(8,128)} %get-tuple-element.334, f32[4,6,128,2048]{3,2,1,0:T(8,128)} %fusion.142, f32[4,6,128]{2,1,0:T(8,128)S(1)} %get-tuple-element.335, f32[4,6,128]{2,1,0:T(8,128)S(1)} %copy-done.18, pred[4,2048]{1,0:T(4,128)(4,1)S(1)} %broadcast_compare_fusion.6), kind=kLoop, calls=%fused_computation.21.clone.1 | loop fusion | flops 37748736 | bytes 62947328 | tf_op jit(solution)/shard_map/while/body/eval_jaxpr/convert_element_type | solution.py:82
  1219.2 5.3 copy.142
  1224.5 9.7 copy.143
  1234.2 8.1 copy.140
  1242.3 9.7 copy.141
  1252.1 10.6 pad_maximum_fusion.6
  1262.7 127.5 %reduce-scatter.3.cloned.1.call-done = bf16[4,8,32,768]{3,1,0,2:T(8,128)(2,1)} async-done(((bf16[4,8,256,768]{3,1,0,2:T(8,128)(2,1)}), bf16[4,8,32,768]{3,1,0,2:T(8,128)(2,1)}) %reduce-scatter.3.cloned.1.call-update) | async-done | bytes 1572880 | tf_op jit(solution)/shard_map/while/body/eval_jaxpr/reduce_scatter | solution.py:103
  1393.7 12.2 fusion.144
  1406.0 12.3 reduce-scatter.5.cloned.1.call-done
  1430.5 5.6 fusion.73
  1438.8 5.5 add_convert_fusion.1
  1446.8 33.9 %all-reduce.2 = (f32[8]{0:T(128)S(1)}, f32[8]{0:T(128)S(1)}) all-reduce(f32[8]{0:T(128)S(1)} %get-tuple-element.160, f32[8]{0:T(128)S(1)} %get-tuple-element.159), channel_id=1, replica_groups=mesh['freq'=2,'tm'=8,'batch'=2] {'freq','tm'}, use_global_device_ids=true, to_apply=%region_45.46 | all-reduce | flops 16 | bytes 128 | tf_op jit(solution)/shard_map/psum | solution.py:253
  1482.6 3.8 multiply_reduce_fusion.2
  1488.9 39.3 %all-reduce = (f32[384]{0:T(512)}, f32[384]{0:T(512)}, f32[384]{0:T(512)}, f32[384]{0:T(512)}, f32[384]{0:T(512)}, /*index=5*/f32[384]{0:T(512)}, f32[384]{0:T(512)}, f32[384]{0:T(512)}, f32[1536]{0:T(1024)}, f32[384]{0:T(512)}) all-reduce(f32[384]{0:T(512)S(1)} %get-tuple-element.223, ...), channel_id=1, replica_groups=mesh['freq'=2,'tm'=8,'batch'=2] {'freq','tm','batch'}, use_global_device_ids=true, to_apply=%region_18.19 | all-reduce | flops 4992 | bytes 39936 | tf_op jit(solution)/shard_map/psum | solution.py:216
  1528.8 75.7 %all-reduce.5.cloned.1.call-done = (f32[384,1152]{1,0:T(8,128)}, f32[384,384]{1,0:T(8,128)}, f32[384,1536]{1,0:T(8,128)}, f32[1536,384]{1,0:T(8,128)}) async-done(((f32[384,1152]{1,0:T(8,128)}, f32[384,384]{1,0:T(8,128)}, f32[384,1536]{1,0:T(8,128)}, f32[1536,384]{1,0:T(8,128)}), (f32[384,1152]{1,0:T(8,128)}, f32[384,384]{1,0:T(8,128)}, f32[384,1536]{1,0:T(8,128)}, ...) | async-done | bytes 7077904 | tf_op jit(solution)/shard_map/psum | solution.py:216
  (250 shorter events, 106.3 us)
Async XLA Ops:
  8.0 473.4 %copy-start = (bf16[384,1536]{1,0:T(8,128)(2,1)S(1)}, bf16[384,1536]{1,0:T(8,128)(2,1)}, u32[]{:S(2)}) copy-start(bf16[384,1536]{1,0:T(8,128)(2,1)} %param.40) | copy-start | bytes 3538948
  12.8 7.0 copy-start.8
  12.9 6.9 copy-start.32
  13.0 6.8 copy-start.30
  13.0 6.8 copy-start.34
  13.8 6.1 copy-start.36
  21.0 4.5 copy-start.47
  26.4 33.0 %all-gather.17.cloned.1.call-start = ((), (), s32[]{:S(2)}) async-start(), calls=%async_computation.3 | async-start | bytes 2359296 | tf_op jit(solution)/shard_map/while/body/eval_jaxpr/all_gather | solution.py:35
  27.5 152.3 %all-gather.19.cloned.1.call-start = ((), (), s32[]{:S(2)}) async-start(), calls=%async_computation.4 | async-start | bytes 14155776 | tf_op jit(solution)/shard_map/while/body/eval_jaxpr/all_gather | solution.py:36
  226.7 12.0 copy-start.3
  252.9 28.5 %all-gather.17.cloned.1.call-start = ((), (), s32[]{:S(2)}) async-start(), calls=%async_computation.3 | async-start | bytes 2359296 | tf_op jit(solution)/shard_map/while/body/eval_jaxpr/all_gather | solution.py:35
  253.8 147.8 %all-gather.19.cloned.1.call-start = ((), (), s32[]{:S(2)}) async-start(), calls=%async_computation.4 | async-start | bytes 14155776 | tf_op jit(solution)/shard_map/while/body/eval_jaxpr/all_gather | solution.py:36
  448.6 12.0 copy-start.3
  475.3 6.0 copy-start.44
  475.4 6.0 copy-start.41
  475.4 6.0 copy-start.45
  481.0 26.7 %copy-start.10 = (f32[1024,384]{1,0:T(8,128)}, f32[1024,384]{1,0:T(8,128)S(1)}, u32[]{:S(2)}) copy-start(f32[1024,384]{1,0:T(8,128)S(1)} %get-tuple-element.228) | copy-start | bytes 4718596
  481.4 16.3 %copy-start.13 = (bf16[8,4,32,384]{3,2,1,0:T(8,128)(2,1)S(1)}, bf16[8,4,32,384]{3,2,1,0:T(8,128)(2,1)}, u32[]{:S(2)}) copy-start(bf16[8,4,32,384]{3,2,1,0:T(8,128)(2,1)} %param.29) | copy-start | bytes 2359300
  481.4 16.3 %copy-start.49 = (bf16[1536,384]{1,0:T(8,128)(2,1)S(1)}, bf16[1536,384]{1,0:T(8,128)(2,1)}, u32[]{:S(2)}) copy-start(bf16[1536,384]{1,0:T(8,128)(2,1)} %param.42) | copy-start | bytes 3538948
  507.6 2.8 copy-start.15
  507.6 4.2 copy-start.22
  508.3 7.3 copy-start.50
  508.4 4.2 copy-start.28
  519.9 157.6 %copy-start.6 = (bf16[2,4,4,32,768]{4,3,1,0,2:T(8,128)(2,1)}, bf16[2,4,4,32,768]{4,3,1,0,2:T(8,128)(2,1)S(1)}, u32[]{:S(2)}) copy-start(bf16[2,4,4,32,768]{4,3,1,0,2:T(8,128)(2,1)S(1)} %get-tuple-element.378) | copy-start | bytes 4718596 | tf_op jit(solution)/shard_map/while
  519.9 180.6 %copy-start.4 = (bf16[2,4,128,6,64]{2,4,3,1,0:T(8,128)(2,1)}, bf16[2,4,128,6,64]{2,4,3,1,0:T(8,128)(2,1)S(1)}, u32[]{:S(2)}) copy-start(bf16[2,4,128,6,64]{2,4,3,1,0:T(8,128)(2,1)S(1)} %get-tuple-element.380) | copy-start | bytes 2359300 | tf_op jit(solution)/shard_map/while
  519.9 28.2 %all-gather.21.cloned.1.call-start = ((), (), s32[]{:S(2)}) async-start(), calls=%async_computation.5 | async-start | bytes 2359296 | tf_op jit(solution)/shard_map/while/body/eval_jaxpr/all_gather | solution.py:40
  521.0 147.4 %all-gather.23.cloned.1.call-start = ((), (), s32[]{:S(2)}) async-start(), calls=%async_computation.6 | async-start | bytes 14155776 | tf_op jit(solution)/shard_map/while/body/eval_jaxpr/all_gather | solution.py:41
  551.5 387.5 %reduce-scatter.3.cloned.1.call-start = ((), (), s32[]{:S(2)}) async-start(), calls=%async_computation.7 | async-start | bytes 14155776 | tf_op jit(solution)/shard_map/while/body/eval_jaxpr/reduce_scatter | solution.py:103
  700.5 14.6 copy-start.18
  763.3 4.6 copy-start.2
  811.4 155.6 %reduce-scatter.5.cloned.1.call-start = ((), (), s32[]{:S(2)}) async-start(), calls=%async_computation.8 | async-start | bytes 2359296 | tf_op jit(solution)/shard_map/while/body/eval_jaxpr/reduce_scatter | solution.py:106
  942.4 26.6 %copy-start.5 = (bf16[2,4,128,6,64]{2,4,3,1,0:T(8,128)(2,1)S(1)}, bf16[2,4,128,6,64]{2,4,3,1,0:T(8,128)(2,1)}, u32[]{:S(2)}) copy-start(bf16[2,4,128,6,64]{2,4,3,1,0:T(8,128)(2,1)} %copy-done.4) | copy-start | bytes 2359300 | tf_op jit(solution)/shard_map/while
  942.5 26.6 %copy-start.7 = (bf16[2,4,4,32,768]{4,3,1,0,2:T(8,128)(2,1)S(1)}, bf16[2,4,4,32,768]{4,3,1,0,2:T(8,128)(2,1)}, u32[]{:S(2)}) copy-start(bf16[2,4,4,32,768]{4,3,1,0,2:T(8,128)(2,1)} %copy-done.6) | copy-start | bytes 4718596 | tf_op jit(solution)/shard_map/while
  969.1 159.7 %copy-start.6 = (bf16[2,4,4,32,768]{4,3,1,0,2:T(8,128)(2,1)}, bf16[2,4,4,32,768]{4,3,1,0,2:T(8,128)(2,1)S(1)}, u32[]{:S(2)}) copy-start(bf16[2,4,4,32,768]{4,3,1,0,2:T(8,128)(2,1)S(1)} %get-tuple-element.378) | copy-start | bytes 4718596 | tf_op jit(solution)/shard_map/while
  969.1 182.7 %copy-start.4 = (bf16[2,4,128,6,64]{2,4,3,1,0:T(8,128)(2,1)}, bf16[2,4,128,6,64]{2,4,3,1,0:T(8,128)(2,1)S(1)}, u32[]{:S(2)}) copy-start(bf16[2,4,128,6,64]{2,4,3,1,0:T(8,128)(2,1)S(1)} %get-tuple-element.380) | copy-start | bytes 2359300 | tf_op jit(solution)/shard_map/while
  969.1 30.3 %all-gather.21.cloned.1.call-start = ((), (), s32[]{:S(2)}) async-start(), calls=%async_computation.5 | async-start | bytes 2359296 | tf_op jit(solution)/shard_map/while/body/eval_jaxpr/all_gather | solution.py:40
  970.2 149.5 %all-gather.23.cloned.1.call-start = ((), (), s32[]{:S(2)}) async-start(), calls=%async_computation.6 | async-start | bytes 14155776 | tf_op jit(solution)/shard_map/while/body/eval_jaxpr/all_gather | solution.py:41
  1002.8 387.5 %reduce-scatter.3.cloned.1.call-start = ((), (), s32[]{:S(2)}) async-start(), calls=%async_computation.7 | async-start | bytes 14155776 | tf_op jit(solution)/shard_map/while/body/eval_jaxpr/reduce_scatter | solution.py:103
  1151.7 14.6 copy-start.18
  1214.6 4.6 copy-start.2
  1262.7 155.6 %reduce-scatter.5.cloned.1.call-start = ((), (), s32[]{:S(2)}) async-start(), calls=%async_computation.8 | async-start | bytes 2359296 | tf_op jit(solution)/shard_map/while/body/eval_jaxpr/reduce_scatter | solution.py:106
  1393.7 26.7 %copy-start.5 = (bf16[2,4,128,6,64]{2,4,3,1,0:T(8,128)(2,1)S(1)}, bf16[2,4,128,6,64]{2,4,3,1,0:T(8,128)(2,1)}, u32[]{:S(2)}) copy-start(bf16[2,4,128,6,64]{2,4,3,1,0:T(8,128)(2,1)} %copy-done.4) | copy-start | bytes 2359300 | tf_op jit(solution)/shard_map/while
  1393.7 26.7 %copy-start.7 = (bf16[2,4,4,32,768]{4,3,1,0,2:T(8,128)(2,1)S(1)}, bf16[2,4,4,32,768]{4,3,1,0,2:T(8,128)(2,1)}, u32[]{:S(2)}) copy-start(bf16[2,4,4,32,768]{4,3,1,0,2:T(8,128)(2,1)} %copy-done.6) | copy-start | bytes 4718596 | tf_op jit(solution)/shard_map/while
  1427.7 176.8 %all-reduce.5.cloned.1.call-start = ((), (), s32[]{:S(2)}) async-start(), calls=%async_computation.2 | async-start | bytes 14155776 | tf_op jit(solution)/shard_map/psum | solution.py:216
  1427.7 8.4 copy-start.17
  1430.5 8.1 copy-start.23
  1430.5 5.6 copy-start.24
  1438.8 7.9 copy-start.27
  1438.8 7.9 copy-start.48
  1438.8 42.0 %copy-start.26 = (pred[8,4,32]{2,1,0:T(4,128)(4,1)S(1)}, pred[8,4,32]{2,1,0:T(4,128)(4,1)}, u32[]{:S(2)}) copy-start(pred[8,4,32]{2,1,0:T(4,128)(4,1)} %copy-done.25) | copy-start | bytes 3076
  1438.8 42.0 %copy-start.19 = (bf16[2,4,128,6,64]{2,4,3,1,0:T(8,128)(2,1)S(1)}, bf16[2,4,128,6,64]{2,4,3,1,0:T(8,128)(2,1)}, u32[]{:S(2)}) copy-start(bf16[2,4,128,6,64]{2,4,3,1,0:T(8,128)(2,1)} %get-tuple-element.95) | copy-start | bytes 2359300
  1438.8 42.3 %copy-start.14 = (bf16[8,4,32,384]{3,2,1,0:T(8,128)(2,1)S(1)}, bf16[8,4,32,384]{3,2,1,0:T(8,128)(2,1)}, u32[]{:S(2)}) copy-start(bf16[8,4,32,384]{3,2,1,0:T(8,128)(2,1)} %param.29) | copy-start | bytes 2359300
  1438.8 43.8 %copy-start.9 = (f32[8,4,32,384]{3,2,1,0:T(8,128)S(1)}, f32[8,4,32,384]{3,2,1,0:T(8,128)}, u32[]{:S(2)}) copy-start(f32[8,4,32,384]{3,2,1,0:T(8,128)} %copy-done.8) | copy-start | bytes 4718596
  1438.8 43.8 %copy-start.33 = (f32[1024]{0:T(1024)S(1)}, f32[1024]{0:T(1024)}, u32[]{:S(2)}) copy-start(f32[1024]{0:T(1024)} %copy-done.32) | copy-start | bytes 12292
  1438.8 43.8 %copy-start.35 = (f32[1024]{0:T(1024)S(1)}, f32[1024]{0:T(1024)}, u32[]{:S(2)}) copy-start(f32[1024]{0:T(1024)} %copy-done.34) | copy-start | bytes 12292
  1438.8 43.8 %copy-start.37 = (f32[384]{0:T(512)S(1)}, f32[384]{0:T(512)}, u32[]{:S(2)}) copy-start(f32[384]{0:T(512)} %copy-done.36) | copy-start | bytes 4612
  1480.8 5.7 copy-start.31
  1482.6 4.6 copy-start.12
  1482.6 4.6 copy-start.29
  1486.4 2.5 copy-start.39
  1486.4 2.5 copy-start.40
  1604.5 4.9 copy-start.21
  1604.5 6.3 copy-start.20
  1604.5 7.7 copy-start.1
  (7 other events, 14.3 us)
Sparse Core Ops, SparseCore 0:
  29.5 29.8 all-gather.16
  63.0 116.7 all-gather.18
  255.9 25.4 all-gather.16
  284.9 116.7 all-gather.18
  522.6 25.4 all-gather.20
  551.6 116.7 all-gather.22
  811.5 127.4 reduce-scatter.2
  942.6 24.3 reduce-scatter.4
  972.1 27.2 all-gather.20
  1002.9 116.7 all-gather.22
  1262.8 127.4 reduce-scatter.2
  1393.8 24.4 reduce-scatter.4
Sparse Core Ops, SparseCore 1:
  1438.7 165.7 all-reduce.4
where the time goes:
time: 1630 us; the launch traced here: 1620 us
  waiting for transfers between devices  934 us (57%)
  local copies, waits for them, and re-layouts  257 us (16%)
  matrix products  230 us (14%)
  other arithmetic  96.1 us (6%)
  blocking collectives  73.2 us (4%)
  between operations  16.4 us (1%)
    reduce_scatter x2, waiting for transfers between devices, attend_backward(): lax.psum_scatter(grad_full.astype(jnp.bfloat16), 'tm', scatter_dimension=...  255 us
    all_gather x2, waiting for transfers between devices, gather_keys(): return lax.all_gather(wider, 'tm', axis=2, tiled=True)  232 us
    all_gather x2, waiting for transfers between devices, gather_again(): return lax.all_gather(wider, 'tm', axis=2, tiled=True)  230 us
    psum x1, waiting for transfers between devices, per_device(): lax.psum((grad_mask_embed, grad_ln1_gain, grad_ln1_shift, grad_w_qkv, gra...  75.7 us
    all_gather x2, waiting for transfers between devices, gather_keys(): wider = lax.all_gather(local, 'freq', axis=1, tiled=True)  59.4 us
    dot_general x4, matrix products, masked_scores(): jnp.einsum('bqhd,bkhd->bhqk', queries, key_rows, preferred_element_type=j...  58.5 us
    all_gather x2, waiting for transfers between devices, gather_again(): wider = lax.all_gather(local, 'freq', axis=1, tiled=True)  56.1 us
    slice x6, local copies, waits for them, and re-layouts, split_heads(): key_rows = flat_rows[:, :, :D].reshape(blocks, -1, HEADS, HEAD_DIM)  46.4 us
  transfers between devices with their start and end apart: 13, of which 13 were waited for; matrix products, arithmetic and copies ran while one was open for 3% of the time, Pallas kernels for 0%

commit v1 on v0

--- a/solution.py
+++ b/solution.py
@@ -213,24 +213,27 @@
     grad_start = grad_middle + grad_start_norm
     grad_mask_embed = jnp.sum(jnp.where(flat_mask, grad_start, 0.0), axis=0)
     input_grad = jnp.where(flat_mask, 0.0, grad_start).astype(jnp.bfloat16).reshape(patches.shape)
-    summed = lax.psum(
-        (
-            grad_mask_embed,
-            grad_ln1_gain,
-            grad_ln1_shift,
-            grad_w_qkv,
-            grad_bias_q,
-            grad_bias_v,
-            grad_w_out,
-            grad_bias_out,
-            grad_ln2_gain,
-            grad_ln2_shift,
-            grad_w_up,
-            grad_bias_up,
-            grad_w_down,
-            grad_bias_down,
+    summed = jax.lax.psum(
+        jax.lax.psum(
+            (
+                grad_mask_embed,
+                grad_ln1_gain,
+                grad_ln1_shift,
+                grad_w_qkv,
+                grad_bias_q,
+                grad_bias_v,
+                grad_w_out,
+                grad_bias_out,
+                grad_ln2_gain,
+                grad_ln2_shift,
+                grad_w_up,
+                grad_bias_up,
+                grad_w_down,
+                grad_bias_down,
+            ),
+            ("tm", "batch"),
         ),
-        ("freq", "tm", "batch"),
+        "freq",
     )
     out_rows = block_out.reshape(clips, clip_rows, width)
     logits = jnp.einsum("cqd,cnd->cqn", out_rows, targets, preferred_element_type=jnp.float32)

time: 1630 us -> 1790 us (1.098)
  waiting for transfers between devices: 934 us -> 1070 us
  blocking collectives: 73.2 us -> 101 us
    psum x1 -> x2, waiting for transfers between devices: 75.7 us -> 209 us  [the longest x1 152 us: per_device(): jax.lax.psum((grad_mask_embed, grad_ln1_gain, grad_ln1_shift, grad_w_qkv,...]
    psum x1 -> x2, blocking collectives: 39.3 us -> 67.6 us  [the longest x1 59 us: per_device(): jax.lax.psum((grad_mask_embed, grad_ln1_gain, grad_ln1_shift, grad_w_qkv,...]
  transfers between devices with their start and end apart: 13 -> 14, of which waited for: 13 -> 14; matrix products, arithmetic and copies ran while one was open for 3% -> 3% of each run, Pallas kernels for 0% -> 0%
where the time goes in v1:
time: 1790 us; the launch traced here: 1780 us
  waiting for transfers between devices  1070 us (60%)
  local copies, waits for them, and re-layouts  257 us (14%)
  matrix products  229 us (13%)
  blocking collectives  101 us (6%)
  other arithmetic  96.1 us (5%)
    reduce_scatter x2, waiting for transfers between devices, attend_backward(): lax.psum_scatter(grad_full.astype(jnp.bfloat16), 'tm', scatter_dimension=...  255 us
    all_gather x2, waiting for transfers between devices, gather_keys(): return lax.all_gather(wider, 'tm', axis=2, tiled=True)  232 us
    all_gather x2, waiting for transfers between devices, gather_again(): return lax.all_gather(wider, 'tm', axis=2, tiled=True)  230 us
    psum x1, waiting for transfers between devices, per_device(): jax.lax.psum((grad_mask_embed, grad_ln1_gain, grad_ln1_shift, grad_w_qkv,...  152 us
    all_gather x2, waiting for transfers between devices, gather_keys(): wider = lax.all_gather(local, 'freq', axis=1, tiled=True)  59.4 us
    psum x1, blocking collectives, per_device(): jax.lax.psum((grad_mask_embed, grad_ln1_gain, grad_ln1_shift, grad_w_qkv,...  59 us
    dot_general x4, matrix products, masked_scores(): jnp.einsum('bqhd,bkhd->bhqk', queries, key_rows, preferred_element_type=j...  58.5 us
    psum x1, waiting for transfers between devices, per_device(): jax.lax.psum(jax.lax.psum((grad_mask_embed, grad_ln1_gain, grad_ln1_shift...  57.2 us
  transfers between devices with their start and end apart: 14, of which 14 were waited for; matrix products, arithmetic and copies ran while one was open for 3% of the time, Pallas kernels for 0%

profile of v1, /device:TPU:0, one launch (start us, length us, event | category | flops | bytes accessed | tf_op | source)
XLA Modules:
  0.0 1780.0 jit_solution(17715394955312094295)
XLA Ops:
  26.1 449.2 %while.24 = (s32[]{:T(128)}, bf16[2,4,128,6,64]{2,1,0,4,3:T(4,128)(2,1)}, f32[2,4,6,128,1]{3,2,1,4,0:T(8,128)}, bf16[2,4,4,32,768]{4,3,1,0,2:T(8,128)(2,1)S(1)},...) while((s32[]{:T(128)}, bf16[2,4,128,6,64]{2,1,0,4,3:T(4,128)(2,1)}, ...), condition=%wide.region_5.6_spmd, body=%wide.region_2.5_spmd.sunk | while | flops 1686311936 | bytes 244748528 | solution.py:160
  27.5 31.9 %all-gather.17.cloned.1.call-done = bf16[1,4,8,32,768]{4,3,1,0,2:T(8,128)(2,1)} async-done(((bf16[1,4,4,32,768]{4,3,1,0,2:T(8,128)(2,1)}), bf16[1,4,8,32,768]{4,3,1,0,2:T(8,128)(2,1)}) %all-gather.17.cloned.1.call-update) | async-done | bytes 1572880 | tf_op jit(solution)/shard_map/while/body/eval_jaxpr/all_gather | solution.py:35
  63.6 116.1 %all-gather.19.cloned.1.call-done = bf16[1,4,8,256,768]{4,2,1,0,3:T(8,128)(2,1)} async-done(((bf16[1,4,8,32,768]{4,2,1,0,3:T(8,128)(2,1)}), bf16[1,4,8,256,768]{4,2,1,0,3:T(8,128)(2,1)}) %all-gather.19.cloned.1.call-update) | async-done | bytes 12582928 | tf_op jit(solution)/shard_map/while/body/eval_jaxpr/all_gather | solution.py:36
  179.7 9.1 copy.128
  188.8 5.9 fusion.127
  194.7 8.6 copy.131
  203.3 8.7 copy.129
  212.0 14.7 fusion.129
  226.7 11.4 fusion.130
  238.7 12.2 fusion.131
  253.9 27.5 %all-gather.17.cloned.1.call-done = bf16[1,4,8,32,768]{4,3,1,0,2:T(8,128)(2,1)} async-done(((bf16[1,4,4,32,768]{4,3,1,0,2:T(8,128)(2,1)}), bf16[1,4,8,32,768]{4,3,1,0,2:T(8,128)(2,1)}) %all-gather.17.cloned.1.call-update) | async-done | bytes 1572880 | tf_op jit(solution)/shard_map/while/body/eval_jaxpr/all_gather | solution.py:35
  285.6 116.1 %all-gather.19.cloned.1.call-done = bf16[1,4,8,256,768]{4,2,1,0,3:T(8,128)(2,1)} async-done(((bf16[1,4,8,32,768]{4,2,1,0,3:T(8,128)(2,1)}), bf16[1,4,8,256,768]{4,2,1,0,3:T(8,128)(2,1)}) %all-gather.19.cloned.1.call-update) | async-done | bytes 12582928 | tf_op jit(solution)/shard_map/while/body/eval_jaxpr/all_gather | solution.py:36
  401.7 9.1 copy.128
  410.8 5.9 fusion.127
  416.6 8.6 copy.131
  425.2 8.7 copy.129
  434.0 14.7 fusion.129
  448.6 11.4 fusion.130
  460.6 12.2 fusion.131
  481.5 16.3 multiply_convert_fusion.2
  515.6 911.9 %while.25 = (s32[]{:T(128)}, bf16[2,4,128,6,64]{2,4,3,1,0:T(8,128)(2,1)}, bf16[2,4,4,32,768]{4,3,2,1,0:T(8,128)(2,1)}, bf16[2,4,4,32,768]{4,3,1,0,2:T(8,128)(2,1...) while((s32[]{:T(128)}, ...), condition=%wide.region_14.15_spmd, body=%wide.region_10.14_spmd.sunk | while | flops 4155905024 | bytes 551883200 | solution.py:202
  521.1 27.0 %all-gather.21.cloned.1.call-done = bf16[1,4,8,32,768]{4,3,1,0,2:T(8,128)(2,1)} async-done(((bf16[1,4,4,32,768]{4,3,1,0,2:T(8,128)(2,1)}), bf16[1,4,8,32,768]{4,3,1,0,2:T(8,128)(2,1)}) %all-gather.21.cloned.1.call-update) | async-done | bytes 1572880 | tf_op jit(solution)/shard_map/while/body/eval_jaxpr/all_gather | solution.py:40
  553.2 115.2 %all-gather.23.cloned.1.call-done = bf16[1,4,8,256,768]{4,2,1,0,3:T(8,128)(2,1)} async-done(((bf16[1,4,8,32,768]{4,2,1,0,3:T(8,128)(2,1)}), bf16[1,4,8,256,768]{4,2,1,0,3:T(8,128)(2,1)}) %all-gather.23.cloned.1.call-update) | async-done | bytes 12582928 | tf_op jit(solution)/shard_map/while/body/eval_jaxpr/all_gather | solution.py:41
  668.4 9.1 copy.136
  677.5 5.6 fusion.141
  683.1 8.7 copy.137
  691.8 8.7 copy.139
  700.5 14.6 fusion.142
  715.0 12.9 fusion.145
  727.9 18.5 %multiply_reduce_fusion.8 = (f32[4,6,128]{2,1,0:T(8,128)S(1)}, f32[4,6,128,2048]{3,2,1,0:T(8,128)}) fusion(f32[4,6,128,2048]{3,2,1,0:T(8,128)} %fusion.142, f32[4,6,128]{2,1,0:T(8,128)S(1)} %copy-done.18, pred[4,2048]{1,0:T(4,128)(4,1)S(1)} %broadcast_compare_fusion.6, bf16[4,2048,6,64]{1,3,2,0:T(8,128)(2,1)} %bitcast.204, ...), kind=kOutput, calls=%fused_computation.22.clone.1 | convolution fusion | flops 836760576 | bytes 57049088 | tf_op jit(solution)/shard_map/while/body/eval_jaxpr/bqhd,bkhd->bhqk/dot_general | solution.py:78
  746.4 16.9 multiply_convert_fusion.5
  767.9 5.3 copy.142
  773.2 9.7 copy.143
  782.9 8.1 copy.140
  791.0 9.7 copy.141
  800.8 10.6 pad_maximum_fusion.6
  811.4 127.6 %reduce-scatter.3.cloned.1.call-done = bf16[4,8,32,768]{3,1,0,2:T(8,128)(2,1)} async-done(((bf16[4,8,256,768]{3,1,0,2:T(8,128)(2,1)}), bf16[4,8,32,768]{3,1,0,2:T(8,128)(2,1)}) %reduce-scatter.3.cloned.1.call-update) | async-done | bytes 1572880 | tf_op jit(solution)/shard_map/while/body/eval_jaxpr/reduce_scatter | solution.py:103
  942.5 12.2 fusion.144
  954.7 12.3 reduce-scatter.5.cloned.1.call-done
  970.3 29.1 %all-gather.21.cloned.1.call-done = bf16[1,4,8,32,768]{4,3,1,0,2:T(8,128)(2,1)} async-done(((bf16[1,4,4,32,768]{4,3,1,0,2:T(8,128)(2,1)}), bf16[1,4,8,32,768]{4,3,1,0,2:T(8,128)(2,1)}) %all-gather.21.cloned.1.call-update) | async-done | bytes 1572880 | tf_op jit(solution)/shard_map/while/body/eval_jaxpr/all_gather | solution.py:40
  1004.5 115.2 %all-gather.23.cloned.1.call-done = bf16[1,4,8,256,768]{4,2,1,0,3:T(8,128)(2,1)} async-done(((bf16[1,4,8,32,768]{4,2,1,0,3:T(8,128)(2,1)}), bf16[1,4,8,256,768]{4,2,1,0,3:T(8,128)(2,1)}) %all-gather.23.cloned.1.call-update) | async-done | bytes 12582928 | tf_op jit(solution)/shard_map/while/body/eval_jaxpr/all_gather | solution.py:41
  1119.7 9.1 copy.136
  1128.8 5.6 fusion.141
  1134.4 8.7 copy.137
  1143.1 8.7 copy.139
  1151.7 14.6 fusion.142
  1166.3 12.9 fusion.145
  1179.2 18.5 %multiply_reduce_fusion.8 = (f32[4,6,128]{2,1,0:T(8,128)S(1)}, f32[4,6,128,2048]{3,2,1,0:T(8,128)}) fusion(f32[4,6,128,2048]{3,2,1,0:T(8,128)} %fusion.142, f32[4,6,128]{2,1,0:T(8,128)S(1)} %copy-done.18, pred[4,2048]{1,0:T(4,128)(4,1)S(1)} %broadcast_compare_fusion.6, bf16[4,2048,6,64]{1,3,2,0:T(8,128)(2,1)} %bitcast.204, ...), kind=kOutput, calls=%fused_computation.22.clone.1 | convolution fusion | flops 836760576 | bytes 57049088 | tf_op jit(solution)/shard_map/while/body/eval_jaxpr/bqhd,bkhd->bhqk/dot_general | solution.py:78
  1197.7 16.9 multiply_convert_fusion.5
  1219.2 5.3 copy.142
  1224.5 9.7 copy.143
  1234.2 8.1 copy.140
  1242.3 9.7 copy.141
  1252.1 10.6 pad_maximum_fusion.6
  1262.7 127.5 %reduce-scatter.3.cloned.1.call-done = bf16[4,8,32,768]{3,1,0,2:T(8,128)(2,1)} async-done(((bf16[4,8,256,768]{3,1,0,2:T(8,128)(2,1)}), bf16[4,8,32,768]{3,1,0,2:T(8,128)(2,1)}) %reduce-scatter.3.cloned.1.call-update) | async-done | bytes 1572880 | tf_op jit(solution)/shard_map/while/body/eval_jaxpr/reduce_scatter | solution.py:103
  1393.7 12.2 fusion.144
  1406.0 12.3 reduce-scatter.5.cloned.1.call-done
  1430.4 5.6 fusion.73
  1438.6 151.5 %all-reduce.8.cloned.1.call-done = (f32[384,1152]{1,0:T(8,128)}, f32[384,384]{1,0:T(8,128)}, f32[384,1536]{1,0:T(8,128)}, f32[1536,384]{1,0:T(8,128)}) async-done(((f32[384,1152]{1,0:T(8,128)}, f32[384,384]{1,0:T(8,128)}, f32[384,1536]{1,0:T(8,128)}, f32[1536,384]{1,0:T(8,128)}), (f32[384,1152]{1,0:T(8,128)}, f32[384,384]{1,0:T(8,128)}, f32[384,1536]{1,0:T(8,128)}, ...) | async-done | bytes 7077904 | tf_op jit(solution)/shard_map/psum | solution.py:217
  1590.3 5.5 add_convert_fusion.1
  1598.1 33.1 %all-reduce.2 = (f32[8]{0:T(128)S(1)}, f32[8]{0:T(128)S(1)}) all-reduce(f32[8]{0:T(128)S(1)} %get-tuple-element.160, f32[8]{0:T(128)S(1)} %get-tuple-element.159), channel_id=1, replica_groups=mesh['freq'=2,'tm'=8,'batch'=2] {'freq','tm'}, use_global_device_ids=true, to_apply=%region_59.60 | all-reduce | flops 16 | bytes 128 | tf_op jit(solution)/shard_map/psum | solution.py:256
  1639.4 59.0 %all-reduce = (f32[384]{0:T(512)S(1)}, f32[384]{0:T(512)S(1)}, f32[384]{0:T(512)S(1)}, f32[384]{0:T(512)S(1)}, f32[384]{0:T(512)S(1)}, /*index=5*/f32[384]{0:T(5...) all-reduce(f32[384]{0:T(512)S(1)} %get-tuple-element.237, ...), channel_id=1, replica_groups=mesh['freq'=2,'tm'=8,'batch'=2] {'tm','batch'}, use_global_device_ids=true, to_apply=%region_18.19 | all-reduce | flops 4992 | bytes 39936 | tf_op jit(solution)/shard_map/psum | solution.py:217
  1698.3 8.7 all-reduce.3
  1707.5 57.2 %all-reduce.10.cloned.1.call-done = (f32[384,1152]{1,0:T(8,128)}, f32[384,384]{1,0:T(8,128)}, f32[384,1536]{1,0:T(8,128)}, f32[1536,384]{1,0:T(8,128)}) async-done(((f32[384,1152]{1,0:T(8,128)}, f32[384,384]{1,0:T(8,128)}, f32[384,1536]{1,0:T(8,128)}, f32[1536,384]{1,0:T(8,128)}), (f32[384,1152]{1,0:T(8,128)}, f32[384,384]{1,0:T(8,128)}, f32[384,1536]{1,0:T(8,128)}, ...) | async-done | bytes 7077904 | tf_op jit(solution)/shard_map/psum | solution.py:216
  (254 shorter events, 114.2 us)
Async XLA Ops:
  8.0 473.4 %copy-start = (bf16[384,1536]{1,0:T(8,128)(2,1)S(1)}, bf16[384,1536]{1,0:T(8,128)(2,1)}, u32[]{:S(2)}) copy-start(bf16[384,1536]{1,0:T(8,128)(2,1)} %param.40) | copy-start | bytes 3538948
  12.8 7.0 copy-start.8
  12.9 6.9 copy-start.32
  13.0 6.8 copy-start.30
  13.0 6.8 copy-start.34
  13.8 6.1 copy-start.36
  21.0 4.5 copy-start.47
  26.4 33.0 %all-gather.17.cloned.1.call-start = ((), (), s32[]{:S(2)}) async-start(), calls=%async_computation.4 | async-start | bytes 2359296 | tf_op jit(solution)/shard_map/while/body/eval_jaxpr/all_gather | solution.py:35
  27.5 152.3 %all-gather.19.cloned.1.call-start = ((), (), s32[]{:S(2)}) async-start(), calls=%async_computation.5 | async-start | bytes 14155776 | tf_op jit(solution)/shard_map/while/body/eval_jaxpr/all_gather | solution.py:36
  226.7 12.0 copy-start.3
  252.9 28.5 %all-gather.17.cloned.1.call-start = ((), (), s32[]{:S(2)}) async-start(), calls=%async_computation.4 | async-start | bytes 2359296 | tf_op jit(solution)/shard_map/while/body/eval_jaxpr/all_gather | solution.py:35
  253.8 147.8 %all-gather.19.cloned.1.call-start = ((), (), s32[]{:S(2)}) async-start(), calls=%async_computation.5 | async-start | bytes 14155776 | tf_op jit(solution)/shard_map/while/body/eval_jaxpr/all_gather | solution.py:36
  448.6 12.0 copy-start.3
  475.3 6.0 copy-start.44
  475.4 6.0 copy-start.41
  475.4 6.0 copy-start.45
  481.0 26.7 %copy-start.10 = (f32[1024,384]{1,0:T(8,128)}, f32[1024,384]{1,0:T(8,128)S(1)}, u32[]{:S(2)}) copy-start(f32[1024,384]{1,0:T(8,128)S(1)} %get-tuple-element.242) | copy-start | bytes 4718596
  481.4 16.3 copy-start.13
  481.4 16.3 copy-start.49
  507.6 4.2 copy-start.22
  508.3 7.3 copy-start.50
  508.4 4.2 copy-start.28
  519.9 157.6 %copy-start.6 = (bf16[2,4,4,32,768]{4,3,1,0,2:T(8,128)(2,1)}, bf16[2,4,4,32,768]{4,3,1,0,2:T(8,128)(2,1)S(1)}, u32[]{:S(2)}) copy-start(bf16[2,4,4,32,768]{4,3,1,0,2:T(8,128)(2,1)S(1)} %get-tuple-element.392) | copy-start | bytes 4718596 | tf_op jit(solution)/shard_map/while
  519.9 180.6 %copy-start.4 = (bf16[2,4,128,6,64]{2,4,3,1,0:T(8,128)(2,1)}, bf16[2,4,128,6,64]{2,4,3,1,0:T(8,128)(2,1)S(1)}, u32[]{:S(2)}) copy-start(bf16[2,4,128,6,64]{2,4,3,1,0:T(8,128)(2,1)S(1)} %get-tuple-element.394) | copy-start | bytes 2359300 | tf_op jit(solution)/shard_map/while
  519.9 28.2 %all-gather.21.cloned.1.call-start = ((), (), s32[]{:S(2)}) async-start(), calls=%async_computation.6 | async-start | bytes 2359296 | tf_op jit(solution)/shard_map/while/body/eval_jaxpr/all_gather | solution.py:40
  521.0 147.4 %all-gather.23.cloned.1.call-start = ((), (), s32[]{:S(2)}) async-start(), calls=%async_computation.7 | async-start | bytes 14155776 | tf_op jit(solution)/shard_map/while/body/eval_jaxpr/all_gather | solution.py:41
  551.5 387.5 %reduce-scatter.3.cloned.1.call-start = ((), (), s32[]{:S(2)}) async-start(), calls=%async_computation.8 | async-start | bytes 14155776 | tf_op jit(solution)/shard_map/while/body/eval_jaxpr/reduce_scatter | solution.py:103
  700.5 14.6 copy-start.18
  763.3 4.6 copy-start.2
  811.4 155.6 %reduce-scatter.5.cloned.1.call-start = ((), (), s32[]{:S(2)}) async-start(), calls=%async_computation.9 | async-start | bytes 2359296 | tf_op jit(solution)/shard_map/while/body/eval_jaxpr/reduce_scatter | solution.py:106
  942.4 26.6 %copy-start.5 = (bf16[2,4,128,6,64]{2,4,3,1,0:T(8,128)(2,1)S(1)}, bf16[2,4,128,6,64]{2,4,3,1,0:T(8,128)(2,1)}, u32[]{:S(2)}) copy-start(bf16[2,4,128,6,64]{2,4,3,1,0:T(8,128)(2,1)} %copy-done.4) | copy-start | bytes 2359300 | tf_op jit(solution)/shard_map/while
  942.5 26.6 %copy-start.7 = (bf16[2,4,4,32,768]{4,3,1,0,2:T(8,128)(2,1)S(1)}, bf16[2,4,4,32,768]{4,3,1,0,2:T(8,128)(2,1)}, u32[]{:S(2)}) copy-start(bf16[2,4,4,32,768]{4,3,1,0,2:T(8,128)(2,1)} %copy-done.6) | copy-start | bytes 4718596 | tf_op jit(solution)/shard_map/while
  969.1 159.7 %copy-start.6 = (bf16[2,4,4,32,768]{4,3,1,0,2:T(8,128)(2,1)}, bf16[2,4,4,32,768]{4,3,1,0,2:T(8,128)(2,1)S(1)}, u32[]{:S(2)}) copy-start(bf16[2,4,4,32,768]{4,3,1,0,2:T(8,128)(2,1)S(1)} %get-tuple-element.392) | copy-start | bytes 4718596 | tf_op jit(solution)/shard_map/while
  969.1 182.7 %copy-start.4 = (bf16[2,4,128,6,64]{2,4,3,1,0:T(8,128)(2,1)}, bf16[2,4,128,6,64]{2,4,3,1,0:T(8,128)(2,1)S(1)}, u32[]{:S(2)}) copy-start(bf16[2,4,128,6,64]{2,4,3,1,0:T(8,128)(2,1)S(1)} %get-tuple-element.394) | copy-start | bytes 2359300 | tf_op jit(solution)/shard_map/while
  969.1 30.3 %all-gather.21.cloned.1.call-start = ((), (), s32[]{:S(2)}) async-start(), calls=%async_computation.6 | async-start | bytes 2359296 | tf_op jit(solution)/shard_map/while/body/eval_jaxpr/all_gather | solution.py:40
  970.2 149.5 %all-gather.23.cloned.1.call-start = ((), (), s32[]{:S(2)}) async-start(), calls=%async_computation.7 | async-start | bytes 14155776 | tf_op jit(solution)/shard_map/while/body/eval_jaxpr/all_gather | solution.py:41
  1002.8 387.5 %reduce-scatter.3.cloned.1.call-start = ((), (), s32[]{:S(2)}) async-start(), calls=%async_computation.8 | async-start | bytes 14155776 | tf_op jit(solution)/shard_map/while/body/eval_jaxpr/reduce_scatter | solution.py:103
  1151.7 14.6 copy-start.18
  1214.6 4.6 copy-start.2
  1262.7 155.6 %reduce-scatter.5.cloned.1.call-start = ((), (), s32[]{:S(2)}) async-start(), calls=%async_computation.9 | async-start | bytes 2359296 | tf_op jit(solution)/shard_map/while/body/eval_jaxpr/reduce_scatter | solution.py:106
  1393.7 26.7 %copy-start.5 = (bf16[2,4,128,6,64]{2,4,3,1,0:T(8,128)(2,1)S(1)}, bf16[2,4,128,6,64]{2,4,3,1,0:T(8,128)(2,1)}, u32[]{:S(2)}) copy-start(bf16[2,4,128,6,64]{2,4,3,1,0:T(8,128)(2,1)} %copy-done.4) | copy-start | bytes 2359300 | tf_op jit(solution)/shard_map/while
  1393.7 26.7 %copy-start.7 = (bf16[2,4,4,32,768]{4,3,1,0,2:T(8,128)(2,1)S(1)}, bf16[2,4,4,32,768]{4,3,1,0,2:T(8,128)(2,1)}, u32[]{:S(2)}) copy-start(bf16[2,4,4,32,768]{4,3,1,0,2:T(8,128)(2,1)} %copy-done.6) | copy-start | bytes 4718596 | tf_op jit(solution)/shard_map/while
  1427.6 162.5 %all-reduce.8.cloned.1.call-start = ((), (), s32[]{:S(2)}) async-start(), calls=%async_computation.2 | async-start | bytes 14155776 | tf_op jit(solution)/shard_map/psum | solution.py:217
  1427.6 8.4 copy-start.17
  1430.4 8.1 copy-start.23
  1430.4 5.6 copy-start.24
  1438.5 151.6 %copy-start.46 = (bf16[384]{0:T(512)(128)(2,1)S(1)}, bf16[384]{0:T(512)(128)(2,1)}, u32[]{:S(2)}) copy-start(bf16[384]{0:T(512)(128)(2,1)} %param.43) | copy-start | bytes 2308
  1438.5 151.6 %copy-start.38 = (s32[8,4,32]{2,1,0:T(4,128)S(1)}, s32[8,4,32]{2,1,0:T(4,128)}, u32[]{:S(2)}) copy-start(s32[8,4,32]{2,1,0:T(4,128)} %param.27) | copy-start | bytes 12292
  1438.5 326.2 %all-reduce.10.cloned.1.call-start = ((), (), s32[]{:S(2)}) async-start(), calls=%async_computation.3 | async-start | bytes 14155776 | tf_op jit(solution)/shard_map/psum | solution.py:216
  1590.2 7.6 copy-start.27
  1590.2 7.6 copy-start.48
  1590.2 40.9 %copy-start.26 = (pred[8,4,32]{2,1,0:T(4,128)(4,1)S(1)}, pred[8,4,32]{2,1,0:T(4,128)(4,1)}, u32[]{:S(2)}) copy-start(pred[8,4,32]{2,1,0:T(4,128)(4,1)} %copy-done.25) | copy-start | bytes 3076
  1590.2 41.0 %copy-start.19 = (bf16[2,4,128,6,64]{2,4,3,1,0:T(8,128)(2,1)S(1)}, bf16[2,4,128,6,64]{2,4,3,1,0:T(8,128)(2,1)}, u32[]{:S(2)}) copy-start(bf16[2,4,128,6,64]{2,4,3,1,0:T(8,128)(2,1)} %get-tuple-element.95) | copy-start | bytes 2359300
  1590.3 41.3 %copy-start.14 = (bf16[8,4,32,384]{3,2,1,0:T(8,128)(2,1)S(1)}, bf16[8,4,32,384]{3,2,1,0:T(8,128)(2,1)}, u32[]{:S(2)}) copy-start(bf16[8,4,32,384]{3,2,1,0:T(8,128)(2,1)} %param.29) | copy-start | bytes 2359300
  1590.3 42.7 %copy-start.9 = (f32[8,4,32,384]{3,2,1,0:T(8,128)S(1)}, f32[8,4,32,384]{3,2,1,0:T(8,128)}, u32[]{:S(2)}) copy-start(f32[8,4,32,384]{3,2,1,0:T(8,128)} %copy-done.8) | copy-start | bytes 4718596
  1590.3 42.7 %copy-start.33 = (f32[1024]{0:T(1024)S(1)}, f32[1024]{0:T(1024)}, u32[]{:S(2)}) copy-start(f32[1024]{0:T(1024)} %copy-done.32) | copy-start | bytes 12292
  1590.3 42.7 %copy-start.35 = (f32[1024]{0:T(1024)S(1)}, f32[1024]{0:T(1024)}, u32[]{:S(2)}) copy-start(f32[1024]{0:T(1024)} %copy-done.34) | copy-start | bytes 12292
  1590.3 42.7 %copy-start.37 = (f32[384]{0:T(512)S(1)}, f32[384]{0:T(512)}, u32[]{:S(2)}) copy-start(f32[384]{0:T(512)} %copy-done.36) | copy-start | bytes 4612
  1631.2 5.7 copy-start.31
  1633.0 4.6 copy-start.12
  1633.0 4.6 copy-start.29
  1764.7 4.9 copy-start.21
  1764.7 6.3 copy-start.20
  1764.7 7.7 copy-start.1
  (8 other events, 17.1 us)
Sparse Core Ops, SparseCore 0:
  29.5 29.8 all-gather.16
  63.0 116.7 all-gather.18
  255.9 25.4 all-gather.16
  284.9 116.7 all-gather.18
  522.6 25.4 all-gather.20
  551.6 116.7 all-gather.22
  811.5 127.4 reduce-scatter.2
  942.6 24.3 reduce-scatter.4
  972.1 27.2 all-gather.20
  1002.9 116.7 all-gather.22
  1262.8 127.4 reduce-scatter.2
  1393.8 24.4 reduce-scatter.4
Sparse Core Ops, SparseCore 1:
  1438.6 151.4 all-reduce.7
  1592.6 172.1 all-reduce.9
